TPU v7x, 32 devices: a whole 2x2x4 slice. The times are simulated.
32 devices in a mesh: span: 2 (over y), tm: 16 (over z, x, core).
Axes of the slice: x: 2, y: 2, z: 4, core: 2. Of those that a mesh axis runs over, the one named last changes fastest.
Arguments:
- traces: bfloat16 [1024, 32768], P(None, ('span', 'tm')), parts along dimension 1, may hold values from -6 to 6
- templates: bfloat16 [256, 16, 512], P('tm'), may hold values from -6 to 6
- blocks: int32 [16, 4], replicated, may hold values from 0 to 7, all different within a row
Outputs:
- detection: float32 [16, 32768], P(None, ('span', 'tm')), parts along dimension 1
There are 2 independent parts, one for each index of `span`. A program takes and returns all parts, laid end to end along the dimension named above; an argument that names none is the same for every part. Nothing has to cross between parts.
Inputs may be any that keep to these rules, and one draw needn't show every extreme that they name: Each row lists 4 different channel blocks.
All inputs are finite; a program needn't handle non-finite values.
Results may differ from a plain program's by a relative error of at most 0.0003.
Values may be sent and summed in bfloat16 or wider, within the bound.
A program may use at most 128 MiB of HBM per device.

v0:
```python
import functools
import math

import jax
import jax.numpy as jnp
from jax import lax
from jax.experimental import pallas as pl
from jax.experimental.pallas import tpu as pltpu
from jax.sharding import PartitionSpec as P

epsilon = 1e-06
MESH = pl.DeviceIdType.MESH


template_groups = 4


def from_behind(block, axis, distance):
    devices = range(lax.axis_size(axis))
    route = [(i - distance, i) for i in devices if i - distance in devices]
    return lax.ppermute(block, axis, route)


def tap_total(product, lag_count):
    members, tap_count, span_width = product.shape
    flattened = product.reshape(members, tap_count * span_width)
    flattened = jnp.pad(flattened, ((0, 0), (0, tap_count)))
    return flattened.reshape(members, tap_count, span_width + 1)[:, :, :lag_count].sum(axis=1)


def plain(traces, templates, blocks):
    channels, lag_count = traces.shape
    local_taps, members, row_count = templates.shape
    listed = blocks.shape[1]
    block_rows = row_count // listed
    nblocks = channels // block_rows
    tap_count = local_taps * lax.axis_size("tm")
    incoming = from_behind(traces[:, :tap_count], "tm", -1)
    source = jnp.concatenate([traces, incoming], axis=1)
    span_width = source.shape[1]
    squares = (
        jnp.square(source.astype(jnp.float32)).reshape(nblocks, block_rows, span_width).sum(axis=1)
    )
    running = jnp.concatenate(
        [jnp.zeros((nblocks, 1), jnp.float32), jnp.cumsum(squares, axis=1)], axis=1
    )
    window = running[:, tap_count : tap_count + lag_count] - running[:, :lag_count]
    selector = (blocks[:, :, None] == jnp.arange(nblocks, dtype=jnp.int32)[None, None, :]).astype(
        jnp.float32
    )
    counting = selector.sum(axis=1)
    scale_factor = math.sqrt(tap_count * row_count)
    group_size = members // template_groups
    gathered = lax.all_gather(templates, "tm", axis=0, tiled=True)
    pieces = []
    norm_pieces = []
    for group_index in range(template_groups):
        offset = group_index * group_size
        weights = gathered[:, offset : offset + group_size]
        chosen = source.reshape(nblocks, block_rows, span_width)[
            blocks[offset : offset + group_size]
        ]
        chosen = chosen.reshape(group_size, row_count, span_width)
        product = jnp.einsum("kqr,qrl->qkl", weights, chosen, preferred_element_type=jnp.float32)
        pieces.append(tap_total(product, lag_count))
        norm_pieces.append(jnp.sum(jnp.square(weights.astype(jnp.float32)), axis=(0, 2)))
    correlation = jnp.concatenate(pieces, axis=0)
    norm_sums = jnp.concatenate(norm_pieces, axis=0)
    energy = jnp.dot(counting, window, precision=lax.Precision.HIGHEST)
    denominator = energy * norm_sums[:, None] + epsilon
    return correlation * lax.rsqrt(denominator) * scale_factor


def only(condition, action):
    @pl.when(condition)
    def _():
        action()


UP, DOWN, ACROSS, PLANE = range(4)


def kernel(
    tm,
    blocks_s, blocks_v, traces, templates, out,
    X, W, S, CP, CC, CN, RC, RN, RP, E, EN,
    x_sem, slab_sem, send_sem, recv_sem, tail_send, tail_recv,
):
    nblocks, depth, lags = traces.shape
    local_taps, members, rows = templates.shape
    listed = blocks_s.shape[1]
    taps = local_taps * tm
    half = members // 2
    pair_taps = 2 * local_taps
    line = tm // 4
    chips = tm // 2
    shared = (3 * half // 4) // 2
    scale = math.sqrt(taps * rows)

    me = lax.axis_index("tm")
    plane = lax.axis_index("span")
    core = lax.rem(me, 2)
    chip = me // 2
    x = lax.rem(chip, 2)
    z = chip // 2

    def device(z_, x_, c_):
        return {"tm": (z_ * 2 + x_) * 2 + c_}

    sibling = device(z, x, 1 - core)
    targets = {
        UP: device(z + 1, x, core),
        DOWN: device(z - 1, x, core),
        ACROSS: device(z, 1 - x, core),
        PLANE: {"span": 1 - plane},
    }
    has_up, has_down = z + 1 < line, z > 0
    has_next, has_prev = chip + 1 < chips, chip > 0

    barrier = pltpu.get_barrier_semaphore()

    def greet(target):
        pl.semaphore_signal(barrier, inc=1, device_id=target, device_id_type=MESH)

    greet(sibling)
    greet(targets[ACROSS])
    greet(targets[PLANE])
    only(has_up, lambda: greet(targets[UP]))
    only(has_down, lambda: greet(targets[DOWN]))

    @pl.when(jnp.logical_and(has_next, core == 1))
    def _():
        greet({"tm": 2 * chip + 2})
        greet({"tm": 2 * chip + 3})

    own_traces = pltpu.make_async_copy(traces, X.at[core], x_sem.at[0])
    own_traces.start()
    S[...] = jnp.swapaxes(templates[...], 0, 1)
    slab_rows = pl.ds(pl.multiple_of(me * local_taps, local_taps), local_taps)
    own_slab = pltpu.make_async_copy(
        S.at[pl.ds(core * half, half)], W.at[:, slab_rows, :], slab_sem.at[0]
    )
    own_slab.start()

    greetings = 3 + has_up.astype(jnp.int32) + has_down.astype(jnp.int32) + has_prev.astype(jnp.int32)
    pl.semaphore_wait(barrier, greetings)

    def remote(src, dst, send, recv, target):
        return pltpu.make_async_remote_copy(
            src_ref=src, dst_ref=dst, send_sem=send, recv_sem=recv,
            device_id=target, device_id_type=MESH,
        )

    other_slab = remote(
        S.at[pl.ds((1 - core) * half, half)], W.at[:, slab_rows, :],
        slab_sem.at[1], slab_sem.at[2], sibling,
    )
    other_slab.start()
    other_traces = remote(traces, X.at[core], x_sem.at[1], x_sem.at[2], sibling)

    started = []

    def move(way, j, p):
        part = W.at[j, pl.ds(pl.multiple_of(p * pair_taps, pair_taps), pair_taps), :]
        return remote(part, part, send_sem.at[way, j, p], recv_sem.at[j, p], targets[way])

    def send(way, j, p, allowed):
        started.append((way, j, p, allowed))
        only(allowed, lambda: move(way, j, p).start())

    def arrived(j, p, allowed):
        only(allowed, lambda: move(ACROSS, j, p).wait_recv())

    own_slab.wait()
    other_slab.wait_recv()

    mine = [plane * shared + i for i in range(shared)]
    theirs = [(1 - plane) * shared + i for i in range(shared)]
    both = list(range(2 * shared, half))
    flows = [(j, True) for j in mine] + [(j, False) for j in both]
    always = z >= 0

    def stage(flow, k):
        j, passed_on = flow
        here = lambda d: (z + d) * 2 + x
        there = lambda d: (z + d) * 2 + 1 - x
        if k == 0:
            send(UP, j, here(0), has_up)
            send(DOWN, j, here(0), has_down)
            send(ACROSS, j, here(0), always)
            return
        if k < line:
            below, above = z >= k, z + k < line
            arrived(j, here(-k), below)
            send(UP, j, here(-k), jnp.logical_and(below, has_up))
            send(ACROSS, j, here(-k), below)
            if passed_on:
                send(PLANE, j, here(-k), below)
            arrived(j, here(k), above)
            send(DOWN, j, here(k), jnp.logical_and(above, has_down))
            send(ACROSS, j, here(k), above)
            if passed_on:
                send(PLANE, j, here(k), above)
        d = k - 1
        if d == 0:
            arrived(j, there(0), always)
            if passed_on:
                send(PLANE, j, there(0), always)
        else:
            below, above = z >= d, z + d < line
            arrived(j, there(-d), below)
            if passed_on:
                send(PLANE, j, there(-d), below)
            arrived(j, there(d), above)
            if passed_on:
                send(PLANE, j, there(d), above)

    def passed(j):
        for d in range(1, chips):
            arrived(j, lax.rem(chip + d, chips), always)

    def correlate(j):
        weights = W[j]
        width = lags + taps
        partial = []
        names = [blocks_s[core * half + j, m] for m in range(listed)]
        half_taps = taps // 2
        for h in range(2):
            chosen = jnp.concatenate([X[h, b] for b in names], axis=0)
            product = jnp.dot(weights, chosen, preferred_element_type=jnp.float32)
            total = None
            for row in range(0, half_taps, 8):
                near = product[row : row + 8]
                far = product[row + half_taps : row + half_taps + 8]
                gap = jnp.zeros((8, half_taps), jnp.float32)
                joined = jnp.concatenate([far, gap], axis=1) + jnp.concatenate([gap, near], axis=1)
                joined = jnp.concatenate([gap, joined], axis=1)
                if row:
                    joined = pltpu.roll(joined, width - row, 1)
                total = joined if total is None else total + joined
            partial.append(total)
        gap = jnp.zeros((8, lags), jnp.float32)
        sheared = jnp.concatenate([partial[0], gap], axis=1) + jnp.concatenate(
            [gap, partial[1]], axis=1
        )
        row_index = lax.broadcasted_iota(jnp.int32, sheared.shape, 0)
        for bit in (1, 2, 4):
            moved = pltpu.roll(sheared, sheared.shape[1] - bit, 1)
            sheared = jnp.where(lax.rem(row_index // bit, 2) == 1, moved, sheared)
        line_sum = jnp.sum(sheared, axis=0, keepdims=True)
        CP[pl.ds(j, 1), :] = line_sum[:, :taps]
        CC[0, pl.ds(j, 1), :] = line_sum[:, taps : taps + lags]
        CC[1, pl.ds(j, 1), :] = line_sum[:, taps + lags :]
        wide = weights.astype(jnp.float32)
        norm = jnp.sum(jnp.sum(wide * wide, axis=0, keepdims=True), axis=1, keepdims=True)
        CN[pl.ds(j, 1), :] = jnp.broadcast_to(norm, (1, CN.shape[1]))

    edge_send = remote(
        E.at[:, pl.ds(0, taps)], E.at[:, pl.ds(lags, taps)],
        tail_send.at[0], tail_recv.at[0], {"tm": me - 1},
    )

    def energies():
        own_traces.wait()
        for b in range(nblocks):
            part = X[core, b].astype(jnp.float32)
            E[pl.ds(b, 1), pl.ds(0, lags)] = jnp.sum(part * part, axis=0, keepdims=True)
        only(me > 0, edge_send.start)

        @pl.when(me + 1 == tm)
        def _():
            E[:, pl.ds(lags, taps)] = jnp.zeros((nblocks, taps), jnp.float32)

    def windows():
        only(me + 1 < tm, edge_send.wait_recv)
        window = E[...]
        reach = 1
        while reach < taps:
            window = window + pltpu.roll(window, window.shape[1] - reach, 1)
            reach *= 2
        window = window[:, :lags]
        table = blocks_v[...]
        energy = jnp.zeros((members, lags), jnp.float32)
        for b in range(nblocks):
            count = jnp.sum((table == b).astype(jnp.float32), axis=1, keepdims=True)
            energy = energy + count * window[b : b + 1]
        EN[...] = energy

    order = {}
    steps = len(flows) + line
    for s in range(steps + 1):
        for i, flow in enumerate(flows):
            if 0 <= s - i <= line:
                stage(flow, s - i)
        if s == 0:
            other_traces.start()
            energies()
        if s == 1:
            windows()
        if s == line - 1:
            other_traces.wait_recv()
        i = s - line
        if 0 <= i < len(flows):
            correlate(flows[i][0])
        if s == steps - 2 and shared:
            passed(theirs[0])
            correlate(theirs[0])
    for j in theirs[1:]:
        passed(j)
        correlate(j)

    mate = remote(CC.at[1 - core], RC, tail_send.at[1], tail_recv.at[1], sibling)
    norms = remote(CN, RN, tail_send.at[2], tail_recv.at[2], sibling)
    before = remote(
        CP, RP.at[core], tail_send.at[3], tail_recv.at[3 + core], {"tm": 2 * chip - 1}
    )
    mate.start()
    norms.start()
    only(has_prev, before.start)
    mate.wait_recv()
    norms.wait_recv()

    mine_rows = pl.ds(pl.multiple_of(core * half, half), half)
    mate_rows = pl.ds(pl.multiple_of((1 - core) * half, half), half)

    takes = jnp.logical_and(has_next, core == 1)

    @pl.when(takes)
    def _():
        for c in range(2):
            remote(CP, RP.at[c], tail_send.at[3], tail_recv.at[3 + c], sibling).wait_recv()

    def finish(value, rows_, norm, tail):
        denominator = EN[rows_, :] * norm[:, :1] + epsilon
        factor = lax.rsqrt(denominator) * scale
        out[rows_, :] = value * factor

        @pl.when(takes)
        def _():
            last = pl.ds(lags - taps, taps)
            out[rows_, last] = (value[:, lags - taps :] + tail()) * factor[:, lags - taps :]

    finish(CC[core], mine_rows, CN[...], lambda: RP[core])
    finish(RC[...], mate_rows, RN[...], lambda: RP[1 - core])

    other_slab.wait_send()
    other_traces.wait_send()
    mate.wait_send()
    norms.wait_send()
    only(has_prev, before.wait_send)
    only(me > 0, edge_send.wait_send)
    for way, j, p, allowed in started:
        only(allowed, move(way, j, p).wait_send)


def fused(traces, templates, blocks):
    channels, lags = traces.shape
    local_taps, members, rows = templates.shape
    tm = lax.axis_size("tm")
    taps = local_taps * tm
    half = members // 2
    depth = rows // blocks.shape[1]
    nblocks = channels // depth
    chips = tm // 2
    vmem = pl.BlockSpec(memory_space=pltpu.VMEM)
    f32 = jnp.float32
    return pl.pallas_call(
        functools.partial(kernel, tm),
        out_shape=jax.ShapeDtypeStruct((members, lags), f32),
        in_specs=[
            pl.BlockSpec(memory_space=pltpu.SMEM),
            vmem,
            pl.BlockSpec(memory_space=pl.ANY),
            vmem,
        ],
        out_specs=vmem,
        scratch_shapes=[
            pltpu.VMEM((2, nblocks, depth, lags), traces.dtype),
            pltpu.VMEM((half, taps, rows), templates.dtype),
            pltpu.VMEM((members, local_taps, rows), templates.dtype),
            pltpu.VMEM((half, taps), f32),
            pltpu.VMEM((2, half, lags), f32),
            pltpu.VMEM((half, 128), f32),
            pltpu.VMEM((half, lags), f32),
            pltpu.VMEM((half, 128), f32),
            pltpu.VMEM((2, half, taps), f32),
            pltpu.VMEM((nblocks, lags + taps), f32),
            pltpu.VMEM((members, lags), f32),
            pltpu.SemaphoreType.DMA((3,)),
            pltpu.SemaphoreType.DMA((3,)),
            pltpu.SemaphoreType.DMA((4, half, chips)),
            pltpu.SemaphoreType.DMA((half, chips)),
            pltpu.SemaphoreType.DMA((4,)),
            pltpu.SemaphoreType.DMA((5,)),
        ],
        compiler_params=pltpu.CompilerParams(
            collective_id=0, has_side_effects=True, vmem_limit_bytes=48 * 2**20
        ),
    )(blocks, blocks, traces.reshape(nblocks, depth, lags), templates)


def per_device(traces, templates, blocks):
    channels, lags = traces.shape
    local_taps, members, rows = templates.shape
    tm = lax.axis_size("tm")
    taps = local_taps * tm
    fits = (
        lax.axis_size("span") == 2
        and tm % 4 == 0
        and local_taps % 16 == 0
        and members == 16
        and taps == 256
        and lags % 128 == 0
        and rows % (128 * blocks.shape[1]) == 0
    )
    return (fused if fits else plain)(traces, templates, blocks)


def solution(mesh):
    return jax.shard_map(
        per_device,
        mesh=mesh,
        in_specs=(P(None, ("span", "tm")), P("tm", None, None), P()),
        out_specs=P(None, ("span", "tm")),
        check_vma=False,
    )
```

profile of v0, /device:TPU:1, one launch (start us, length us, event | category | flops | bytes accessed | tf_op | source)
XLA Modules:
  0.0 44.6 jit_solution(15096226925972465112)
XLA Ops:
  0.0 0.8 %copy.4.blocks_s.blocks_v = s32[16,4]{1,0:T(8,128)S(1)} copy(s32[16,4]{0,1:T(4,128)} %param.5) | data formatting | bytes 512 | tf_op args[2]
  0.8 0.0 copy-start
  0.8 1.6 %copy-done = bf16[1024,1024]{1,0:T(8,128)(2,1)S(1)} copy-done((bf16[1024,1024]{1,0:T(8,128)(2,1)S(1)}, bf16[1024,1024]{1,0:T(8,128)(2,1)}, u32[]{:S(2)}) %copy-start) | copy-done | bytes 2097176
  2.4 0.0 copy-start.1
  2.4 0.9 %copy-done.1 = bf16[16,16,512]{2,1,0:T(8,128)(2,1)S(1)} copy-done((bf16[16,16,512]{2,1,0:T(8,128)(2,1)S(1)}, bf16[16,16,512]{2,1,0:T(8,128)(2,1)}, u32[]{:S(2)}) %copy-start.1) | copy-done | bytes 262168
  3.3 40.6 %shard_map.37 = f32[16,1024]{1,0:T(8,128)S(1)} custom-call(s32[16,4]{1,0:T(8,128)S(1)} %copy.4.blocks_s.blocks_v, s32[16,4]{1,0:T(8,128)S(1)} %copy.4.blocks_s.blocks_v, bf16[8,128,1024]{2,1,0:T(8,128)(2,1)S(1)} %bitcast.1, bf16[16,16,512]{2,1,0:T(8,128)(2,1)S(1)} %copy-done.1), custom_call_target="tpu_custom_call" | custom-call | tf_op jit(solution)/shard_map/pallas_call | solution.py:367
  43.9 0.6 %copy.7 = f32[16,1024]{1,0:T(8,128)} copy(f32[16,1024]{1,0:T(8,128)S(1)} %shard_map.37) | data formatting | bytes 131072
Async XLA Ops:
  0.8 1.6 %copy-start = (bf16[1024,1024]{1,0:T(8,128)(2,1)S(1)}, bf16[1024,1024]{1,0:T(8,128)(2,1)}, u32[]{:S(2)}) copy-start(bf16[1024,1024]{1,0:T(8,128)(2,1)} %param.3) | copy-start | bytes 6291460
  2.4 0.9 %copy-start.1 = (bf16[16,16,512]{2,1,0:T(8,128)(2,1)S(1)}, bf16[16,16,512]{2,1,0:T(8,128)(2,1)}, u32[]{:S(2)}) copy-start(bf16[16,16,512]{2,1,0:T(8,128)(2,1)} %templates.1) | copy-start | bytes 786436
where the time goes:
time: 44.8 us; the launch traced here: 44.6 us
  Pallas kernels  40.6 us (91%)
  local copies, waits for them, and re-layouts  3.93 us (9%)
    pallas_call x1, Pallas kernels, fused(): pl.pallas_call(functools.partial(kernel, tm), out_shape=jax.ShapeDtypeStr...  40.6 us
    unnamed x6, local copies, waits for them, and re-layouts  3.93 us

commit v1 on v0

--- a/solution.py
+++ b/solution.py
@@ -82,13 +82,13 @@
 
 def kernel(
     tm,
-    blocks_s, blocks_v, traces, templates, out,
-    X, W, S, CP, CC, CN, RC, RN, RP, E, EN,
-    x_sem, slab_sem, send_sem, recv_sem, tail_send, tail_recv,
+    listing, traces, templates, out,
+    T, X, W, S, CP, CC, CN, RC, RN, RP, E, WIN, EN,
+    t_sem, x_sem, slab_sem, send_sem, recv_sem, tail_send, tail_recv,
 ):
     nblocks, depth, lags = traces.shape
     local_taps, members, rows = templates.shape
-    listed = blocks_s.shape[1]
+    listed = listing.shape[0]
     taps = local_taps * tm
     half = members // 2
     pair_taps = 2 * local_taps
@@ -117,6 +117,9 @@
     has_up, has_down = z + 1 < line, z > 0
     has_next, has_prev = chip + 1 < chips, chip > 0
 
+    own_templates = pltpu.make_async_copy(templates, T, t_sem)
+    own_templates.start()
+
     barrier = pltpu.get_barrier_semaphore()
 
     def greet(target):
@@ -135,7 +138,8 @@
 
     own_traces = pltpu.make_async_copy(traces, X.at[core], x_sem.at[0])
     own_traces.start()
-    S[...] = jnp.swapaxes(templates[...], 0, 1)
+    own_templates.wait()
+    S[...] = jnp.swapaxes(T[...], 0, 1)
     slab_rows = pl.ds(pl.multiple_of(me * local_taps, local_taps), local_taps)
     own_slab = pltpu.make_async_copy(
         S.at[pl.ds(core * half, half)], W.at[:, slab_rows, :], slab_sem.at[0]
@@ -223,7 +227,7 @@
         weights = W[j]
         width = lags + taps
         partial = []
-        names = [blocks_s[core * half + j, m] for m in range(listed)]
+        names = [listing[m, core * half + j] for m in range(listed)]
         half_taps = taps // 2
         for h in range(2):
             chosen = jnp.concatenate([X[h, b] for b in names], axis=0)
@@ -278,34 +282,40 @@
         while reach < taps:
             window = window + pltpu.roll(window, window.shape[1] - reach, 1)
             reach *= 2
-        window = window[:, :lags]
-        table = blocks_v[...]
-        energy = jnp.zeros((members, lags), jnp.float32)
         for b in range(nblocks):
-            count = jnp.sum((table == b).astype(jnp.float32), axis=1, keepdims=True)
-            energy = energy + count * window[b : b + 1]
-        EN[...] = energy
-
-    order = {}
-    steps = len(flows) + line
-    for s in range(steps + 1):
-        for i, flow in enumerate(flows):
-            if 0 <= s - i <= line:
-                stage(flow, s - i)
-        if s == 0:
-            other_traces.start()
-            energies()
-        if s == 1:
+            WIN[b] = window[b : b + 1, :lags]
+        for j in range(members):
+            energy = WIN[listing[0, j]]
+            for m in range(1, listed):
+                energy = energy + WIN[listing[m, j]]
+            EN[pl.ds(j, 1), :] = energy
+
+    first, second = flows[:shared], flows[shared:]
+
+    def stages(group, k):
+        for flow in group:
+            stage(flow, k)
+
+    stages(first, 0)
+    stages(second, 0)
+    other_traces.start()
+    energies()
+    for k in range(1, line):
+        stages(first, k)
+        if k < line - 1:
+            stages(second, k)
+        if k == 1:
             windows()
-        if s == line - 1:
-            other_traces.wait_recv()
-        i = s - line
-        if 0 <= i < len(flows):
-            correlate(flows[i][0])
-        if s == steps - 2 and shared:
-            passed(theirs[0])
-            correlate(theirs[0])
-    for j in theirs[1:]:
+    stages(first, line)
+    other_traces.wait_recv()
+    for i, flow in enumerate(first):
+        correlate(flow[0])
+        if i == 0:
+            stages(second, line - 1)
+    stages(second, line)
+    for flow in second:
+        correlate(flow[0])
+    for j in theirs:
         passed(j)
         correlate(j)
 
@@ -369,12 +379,12 @@
         out_shape=jax.ShapeDtypeStruct((members, lags), f32),
         in_specs=[
             pl.BlockSpec(memory_space=pltpu.SMEM),
-            vmem,
             pl.BlockSpec(memory_space=pl.ANY),
-            vmem,
+            pl.BlockSpec(memory_space=pl.ANY),
         ],
         out_specs=vmem,
         scratch_shapes=[
+            pltpu.VMEM(templates.shape, templates.dtype),
             pltpu.VMEM((2, nblocks, depth, lags), traces.dtype),
             pltpu.VMEM((half, taps, rows), templates.dtype),
             pltpu.VMEM((members, local_taps, rows), templates.dtype),
@@ -385,7 +395,9 @@
             pltpu.VMEM((half, 128), f32),
             pltpu.VMEM((2, half, taps), f32),
             pltpu.VMEM((nblocks, lags + taps), f32),
+            pltpu.VMEM((nblocks, 1, lags), f32),
             pltpu.VMEM((members, lags), f32),
+            pltpu.SemaphoreType.DMA,
             pltpu.SemaphoreType.DMA((3,)),
             pltpu.SemaphoreType.DMA((3,)),
             pltpu.SemaphoreType.DMA((4, half, chips)),
@@ -394,9 +406,9 @@
             pltpu.SemaphoreType.DMA((5,)),
         ],
         compiler_params=pltpu.CompilerParams(
-            collective_id=0, has_side_effects=True, vmem_limit_bytes=48 * 2**20
+            collective_id=0, has_side_effects=True, vmem_limit_bytes=60 * 2**20
         ),
-    )(blocks, blocks, traces.reshape(nblocks, depth, lags), templates)
+    )(blocks.T, traces.reshape(nblocks, depth, lags), templates)
 
 
 def per_device(traces, templates, blocks):

time: 44.8 us -> 36.7 us (0.82)
  Pallas kernels: 40.6 us -> 35.1 us
  local copies, waits for them, and re-layouts: 3.93 us -> 1.47 us
    pallas_call x1, Pallas kernels: 40.6 us -> 35.1 us  [fused(): pl.pallas_call(functools.partial(kernel, tm), out_shape=jax.ShapeDtypeStr...]
    unnamed x6 -> x1, local copies, waits for them, and re-layouts: 3.93 us -> 1.47 us
where the time goes in v1:
time: 36.7 us; the launch traced here: 36.5 us
  Pallas kernels  35.1 us (96%)
  local copies, waits for them, and re-layouts  1.47 us (4%)
    pallas_call x1, Pallas kernels, fused(): pl.pallas_call(functools.partial(kernel, tm), out_shape=jax.ShapeDtypeStr...  35.1 us
    unnamed x1, local copies, waits for them, and re-layouts  1.47 us

profile of v1, /device:TPU:1, one launch (start us, length us, event | category | flops | bytes accessed | tf_op | source)
XLA Modules:
  0.0 36.5 jit_solution(6254779359817857632)
XLA Ops:
  0.0 35.1 %shard_map.37 = f32[16,1024]{1,0:T(8,128)} custom-call(s32[4,16]{1,0:T(4,128)} %bitcast.3, bf16[8,128,1024]{2,1,0:T(8,128)(2,1)} %bitcast.2, bf16[16,16,512]{2,1,0:T(8,128)(2,1)} %templates.1), custom_call_target="tpu_custom_call" | custom-call | tf_op jit(solution)/shard_map/pallas_call | solution.py:377
  35.1 1.5 %copy.5 = f32[16,1024]{1,0:T(8,128)} copy(f32[16,1024]{1,0:T(8,128)} %shard_map.37) | data formatting | bytes 131072

commit v2 on v1

--- a/solution.py
+++ b/solution.py
@@ -72,6 +72,10 @@
 
 
 def only(condition, action):
+    if condition is None:
+        action()
+        return
+
     @pl.when(condition)
     def _():
         action()
@@ -83,7 +87,7 @@
 def kernel(
     tm,
     listing, traces, templates, out,
-    T, X, W, S, CP, CC, CN, RC, RN, RP, E, WIN, EN,
+    T, X, W, S, CP, CC, CN, RC, RN, RP, E, WIN, EN, PA, PB,
     t_sem, x_sem, slab_sem, send_sem, recv_sem, tail_send, tail_recv,
 ):
     nblocks, depth, lags = traces.shape
@@ -182,7 +186,7 @@
     theirs = [(1 - plane) * shared + i for i in range(shared)]
     both = list(range(2 * shared, half))
     flows = [(j, True) for j in mine] + [(j, False) for j in both]
-    always = z >= 0
+    always = None
 
     def stage(flow, k):
         j, passed_on = flow
@@ -223,30 +227,35 @@
         for d in range(1, chips):
             arrived(j, lax.rem(chip + d, chips), always)
 
-    def correlate(j):
-        weights = W[j]
-        width = lags + taps
-        partial = []
+    tile = 256
+    half_taps = taps // 2
+    pieces = lags // tile
+    bands = half_taps // 8 // pieces
+    unit = {"count": 0, "open": None, "partial": []}
+
+    def multiply(j, h, n, slot):
         names = [listing[m, core * half + j] for m in range(listed)]
-        half_taps = taps // 2
-        for h in range(2):
-            chosen = jnp.concatenate([X[h, b] for b in names], axis=0)
-            product = jnp.dot(weights, chosen, preferred_element_type=jnp.float32)
-            total = None
-            for row in range(0, half_taps, 8):
-                near = product[row : row + 8]
-                far = product[row + half_taps : row + half_taps + 8]
-                gap = jnp.zeros((8, half_taps), jnp.float32)
-                joined = jnp.concatenate([far, gap], axis=1) + jnp.concatenate([gap, near], axis=1)
-                joined = jnp.concatenate([gap, joined], axis=1)
-                if row:
-                    joined = pltpu.roll(joined, width - row, 1)
-                total = joined if total is None else total + joined
-            partial.append(total)
+        chosen = jnp.concatenate([X[h, b, :, pl.ds(n * tile, tile)] for b in names], axis=0)
+        slot[:, pl.ds(n * tile, tile)] = jnp.dot(W[j], chosen, preferred_element_type=jnp.float32)
+
+    def shear(n, slot, total):
+        for band in range(n * bands, (n + 1) * bands):
+            row = 8 * band
+            near = slot[pl.ds(row, 8), :]
+            far = slot[pl.ds(row + half_taps, 8), :]
+            gap = jnp.zeros((8, half_taps), jnp.float32)
+            joined = jnp.concatenate([far, gap], axis=1) + jnp.concatenate([gap, near], axis=1)
+            joined = jnp.concatenate([gap, joined], axis=1)
+            if row:
+                joined = pltpu.roll(joined, joined.shape[1] - row, 1)
+            total = joined if total is None else total + joined
+        return total
+
+    def store(j):
         gap = jnp.zeros((8, lags), jnp.float32)
-        sheared = jnp.concatenate([partial[0], gap], axis=1) + jnp.concatenate(
-            [gap, partial[1]], axis=1
-        )
+        low, high = unit["partial"]
+        unit["partial"] = []
+        sheared = jnp.concatenate([low, gap], axis=1) + jnp.concatenate([gap, high], axis=1)
         row_index = lax.broadcasted_iota(jnp.int32, sheared.shape, 0)
         for bit in (1, 2, 4):
             moved = pltpu.roll(sheared, sheared.shape[1] - bit, 1)
@@ -255,9 +264,29 @@
         CP[pl.ds(j, 1), :] = line_sum[:, :taps]
         CC[0, pl.ds(j, 1), :] = line_sum[:, taps : taps + lags]
         CC[1, pl.ds(j, 1), :] = line_sum[:, taps + lags :]
-        wide = weights.astype(jnp.float32)
+
+    def advance(new):
+        old = unit["open"]
+        slots = (PA, PB) if unit["count"] % 2 == 0 else (PB, PA)
+        total = None
+        for n in range(pieces):
+            if new is not None:
+                multiply(*new, n, slots[0])
+            if old is not None:
+                total = shear(n, slots[1], total)
+        if old is not None:
+            unit["partial"].append(total)
+            if old[1] == 1:
+                store(old[0])
+        unit["open"] = new
+        unit["count"] += 1
+
+    def correlate(j):
+        advance((j, 0))
+        wide = W[j].astype(jnp.float32)
         norm = jnp.sum(jnp.sum(wide * wide, axis=0, keepdims=True), axis=1, keepdims=True)
         CN[pl.ds(j, 1), :] = jnp.broadcast_to(norm, (1, CN.shape[1]))
+        advance((j, 1))
 
     edge_send = remote(
         E.at[:, pl.ds(0, taps)], E.at[:, pl.ds(lags, taps)],
@@ -318,6 +347,7 @@
     for j in theirs:
         passed(j)
         correlate(j)
+    advance(None)
 
     mate = remote(CC.at[1 - core], RC, tail_send.at[1], tail_recv.at[1], sibling)
     norms = remote(CN, RN, tail_send.at[2], tail_recv.at[2], sibling)
@@ -397,6 +427,8 @@
             pltpu.VMEM((nblocks, lags + taps), f32),
             pltpu.VMEM((nblocks, 1, lags), f32),
             pltpu.VMEM((members, lags), f32),
+            pltpu.VMEM((taps, lags), f32),
+            pltpu.VMEM((taps, lags), f32),
             pltpu.SemaphoreType.DMA,
             pltpu.SemaphoreType.DMA((3,)),
             pltpu.SemaphoreType.DMA((3,)),
@@ -422,7 +454,8 @@
         and local_taps % 16 == 0
         and members == 16
         and taps == 256
-        and lags % 128 == 0
+        and lags % 256 == 0
+        and (taps // 16) % (lags // 256) == 0
         and rows % (128 * blocks.shape[1]) == 0
     )
     return (fused if fits else plain)(traces, templates, blocks)

time: 36.7 us -> 35.4 us (0.965)
  Pallas kernels: 35.1 us -> 33.8 us
    pallas_call x1, Pallas kernels: 35.1 us -> 33.8 us  [fused(): pl.pallas_call(functools.partial(kernel, tm), out_shape=jax.ShapeDtypeStr...]
where the time goes in v2:
time: 35.4 us; the launch traced here: 35.2 us
  Pallas kernels  33.8 us (95%)
  local copies, waits for them, and re-layouts  1.47 us (4%)
    pallas_call x1, Pallas kernels, fused(): pl.pallas_call(functools.partial(kernel, tm), out_shape=jax.ShapeDtypeStr...  33.8 us
    unnamed x1, local copies, waits for them, and re-layouts  1.47 us

profile of v2, /device:TPU:1, one launch (start us, length us, event | category | flops | bytes accessed | tf_op | source)
XLA Modules:
  0.0 35.2 jit_solution(11707100492711449223)
XLA Ops:
  0.0 33.8 %shard_map.37 = f32[16,1024]{1,0:T(8,128)} custom-call(s32[4,16]{1,0:T(4,128)} %bitcast.3, bf16[8,128,1024]{2,1,0:T(8,128)(2,1)} %bitcast.2, bf16[16,16,512]{2,1,0:T(8,128)(2,1)} %templates.1), custom_call_target="tpu_custom_call" | custom-call | tf_op jit(solution)/shard_map/pallas_call | solution.py:407
  33.8 1.5 %copy.5 = f32[16,1024]{1,0:T(8,128)} copy(f32[16,1024]{1,0:T(8,128)} %shard_map.37) | data formatting | bytes 131072

commit v3 on v2

--- a/solution.py
+++ b/solution.py
@@ -168,28 +168,31 @@
 
     started = []
 
-    def move(way, j, p):
-        part = W.at[j, pl.ds(pl.multiple_of(p * pair_taps, pair_taps), pair_taps), :]
-        return remote(part, part, send_sem.at[way, j, p], recv_sem.at[j, p], targets[way])
-
-    def send(way, j, p, allowed):
-        started.append((way, j, p, allowed))
-        only(allowed, lambda: move(way, j, p).start())
-
-    def arrived(j, p, allowed):
-        only(allowed, lambda: move(ACROSS, j, p).wait_recv())
+    first = (plane * shared, shared, plane, True)
+    theirs = ((1 - plane) * shared, shared, 1 - plane, False)
+    second = (2 * shared, half - 2 * shared, 2, False)
+
+    def move(way, group, p):
+        start, count, mark, _ = group
+        part = W.at[
+            pl.ds(start, count), pl.ds(pl.multiple_of(p * pair_taps, pair_taps), pair_taps), :
+        ]
+        return remote(part, part, send_sem.at[way, mark, p], recv_sem.at[mark, p], targets[way])
+
+    def send(way, group, p, allowed):
+        started.append((way, group, p, allowed))
+        only(allowed, lambda: move(way, group, p).start())
+
+    def arrived(group, p, allowed):
+        only(allowed, lambda: move(ACROSS, group, p).wait_recv())
 
     own_slab.wait()
     other_slab.wait_recv()
 
-    mine = [plane * shared + i for i in range(shared)]
-    theirs = [(1 - plane) * shared + i for i in range(shared)]
-    both = list(range(2 * shared, half))
-    flows = [(j, True) for j in mine] + [(j, False) for j in both]
     always = None
 
-    def stage(flow, k):
-        j, passed_on = flow
+    def stage(j, k):
+        passed_on = j[3]
         here = lambda d: (z + d) * 2 + x
         there = lambda d: (z + d) * 2 + 1 - x
         if k == 0:
@@ -319,34 +322,28 @@
                 energy = energy + WIN[listing[m, j]]
             EN[pl.ds(j, 1), :] = energy
 
-    first, second = flows[:shared], flows[shared:]
-
-    def stages(group, k):
-        for flow in group:
-            stage(flow, k)
-
-    stages(first, 0)
-    stages(second, 0)
+    stage(first, 0)
+    stage(second, 0)
     other_traces.start()
     energies()
     for k in range(1, line):
-        stages(first, k)
+        stage(first, k)
         if k < line - 1:
-            stages(second, k)
+            stage(second, k)
         if k == 1:
             windows()
-    stages(first, line)
+    stage(first, line)
     other_traces.wait_recv()
-    for i, flow in enumerate(first):
-        correlate(flow[0])
+    for i in range(shared):
+        correlate(first[0] + i)
         if i == 0:
-            stages(second, line - 1)
-    stages(second, line)
-    for flow in second:
-        correlate(flow[0])
-    for j in theirs:
-        passed(j)
-        correlate(j)
+            stage(second, line - 1)
+    stage(second, line)
+    for i in range(second[1]):
+        correlate(second[0] + i)
+    passed(theirs)
+    for i in range(shared):
+        correlate(theirs[0] + i)
     advance(None)
 
     mate = remote(CC.at[1 - core], RC, tail_send.at[1], tail_recv.at[1], sibling)
@@ -432,8 +429,8 @@
             pltpu.SemaphoreType.DMA,
             pltpu.SemaphoreType.DMA((3,)),
             pltpu.SemaphoreType.DMA((3,)),
-            pltpu.SemaphoreType.DMA((4, half, chips)),
-            pltpu.SemaphoreType.DMA((half, chips)),
+            pltpu.SemaphoreType.DMA((4, 3, chips)),
+            pltpu.SemaphoreType.DMA((3, chips)),
             pltpu.SemaphoreType.DMA((4,)),
             pltpu.SemaphoreType.DMA((5,)),
         ],

time: 35.4 us -> 36.9 us (1.042)
  Pallas kernels: 33.8 us -> 35.2 us
    pallas_call x1, Pallas kernels: 33.8 us -> 35.2 us  [fused(): pl.pallas_call(functools.partial(kernel, tm), out_shape=jax.ShapeDtypeStr...]
where the time goes in v3:
time: 36.9 us; the launch traced here: 36.7 us
  Pallas kernels  35.2 us (95%)
  local copies, waits for them, and re-layouts  1.47 us (4%)
    pallas_call x1, Pallas kernels, fused(): pl.pallas_call(functools.partial(kernel, tm), out_shape=jax.ShapeDtypeStr...  35.2 us
    unnamed x1, local copies, waits for them, and re-layouts  1.47 us

profile of v3, /device:TPU:1, one launch (start us, length us, event | category | flops | bytes accessed | tf_op | source)
XLA Modules:
  0.0 36.7 jit_solution(5208962436217636707)
XLA Ops:
  0.0 35.2 %shard_map.37 = f32[16,1024]{1,0:T(8,128)} custom-call(s32[4,16]{1,0:T(4,128)} %bitcast.3, bf16[8,128,1024]{2,1,0:T(8,128)(2,1)} %bitcast.2, bf16[16,16,512]{2,1,0:T(8,128)(2,1)} %templates.1), custom_call_target="tpu_custom_call" | custom-call | tf_op jit(solution)/shard_map/pallas_call | solution.py:404
  35.2 1.5 %copy.5 = f32[16,1024]{1,0:T(8,128)} copy(f32[16,1024]{1,0:T(8,128)} %shard_map.37) | data formatting | bytes 131072

commit v4 on v2

--- a/solution.py
+++ b/solution.py
@@ -281,8 +281,10 @@
         unit["open"] = new
         unit["count"] += 1
 
-    def correlate(j):
+    def correlate(j, between=None):
         advance((j, 0))
+        if between is not None:
+            between()
         wide = W[j].astype(jnp.float32)
         norm = jnp.sum(jnp.sum(wide * wide, axis=0, keepdims=True), axis=1, keepdims=True)
         CN[pl.ds(j, 1), :] = jnp.broadcast_to(norm, (1, CN.shape[1]))
@@ -326,21 +328,24 @@
             stage(flow, k)
 
     stages(first, 0)
-    stages(second, 0)
     other_traces.start()
     energies()
-    for k in range(1, line):
+    stages(first, 1)
+    stages(second, 0)
+    for k in range(2, line):
         stages(first, k)
-        if k < line - 1:
-            stages(second, k)
-        if k == 1:
+        stages(second, k - 1)
+        if k == 2:
             windows()
-    stages(first, line)
     other_traces.wait_recv()
+    stages(first[:1], line)
+
+    def rest():
+        stages(second, line - 1)
+        stages(first[1:], line)
+
     for i, flow in enumerate(first):
-        correlate(flow[0])
-        if i == 0:
-            stages(second, line - 1)
+        correlate(flow[0], rest if i == 0 else None)
     stages(second, line)
     for flow in second:
         correlate(flow[0])

time: 35.4 us -> 37.1 us (1.048)
  Pallas kernels: 33.8 us -> 35.4 us
    pallas_call x1, Pallas kernels: 33.8 us -> 35.4 us  [fused(): pl.pallas_call(functools.partial(kernel, tm), out_shape=jax.ShapeDtypeStr...]
where the time goes in v4:
time: 37.1 us; the launch traced here: 36.9 us
  Pallas kernels  35.4 us (95%)
  local copies, waits for them, and re-layouts  1.47 us (4%)
    pallas_call x1, Pallas kernels, fused(): pl.pallas_call(functools.partial(kernel, tm), out_shape=jax.ShapeDtypeStr...  35.4 us
    unnamed x1, local copies, waits for them, and re-layouts  1.47 us

profile of v4, /device:TPU:1, one launch (start us, length us, event | category | flops | bytes accessed | tf_op | source)
XLA Modules:
  0.0 36.9 jit_solution(11423158626991465589)
XLA Ops:
  0.0 35.4 %shard_map.37 = f32[16,1024]{1,0:T(8,128)} custom-call(s32[4,16]{1,0:T(4,128)} %bitcast.3, bf16[8,128,1024]{2,1,0:T(8,128)(2,1)} %bitcast.2, bf16[16,16,512]{2,1,0:T(8,128)(2,1)} %templates.1), custom_call_target="tpu_custom_call" | custom-call | tf_op jit(solution)/shard_map/pallas_call | solution.py:412
  35.4 1.5 %copy.5 = f32[16,1024]{1,0:T(8,128)} copy(f32[16,1024]{1,0:T(8,128)} %shard_map.37) | data formatting | bytes 131072

commit v5 on v2

--- a/solution.py
+++ b/solution.py
@@ -164,7 +164,15 @@
         slab_sem.at[1], slab_sem.at[2], sibling,
     )
     other_slab.start()
-    other_traces = remote(traces, X.at[core], x_sem.at[1], x_sem.at[2], sibling)
+    other_traces = [
+        remote(traces.at[b], X.at[core, b], x_sem.at[1 + b], x_sem.at[1 + nblocks + b], sibling)
+        for b in range(nblocks)
+    ]
+
+    def share(k):
+        for b in range(k * nblocks // line, (k + 1) * nblocks // line):
+            other_traces[b].start()
+
 
     started = []
 
@@ -327,16 +335,16 @@
 
     stages(first, 0)
     stages(second, 0)
-    other_traces.start()
+    share(0)
     energies()
     for k in range(1, line):
         stages(first, k)
         if k < line - 1:
             stages(second, k)
-        if k == 1:
-            windows()
+        share(k)
     stages(first, line)
-    other_traces.wait_recv()
+    for copy in other_traces:
+        copy.wait_recv()
     for i, flow in enumerate(first):
         correlate(flow[0])
         if i == 0:
@@ -344,6 +352,7 @@
     stages(second, line)
     for flow in second:
         correlate(flow[0])
+    windows()
     for j in theirs:
         passed(j)
         correlate(j)
@@ -384,7 +393,8 @@
     finish(RC[...], mate_rows, RN[...], lambda: RP[1 - core])
 
     other_slab.wait_send()
-    other_traces.wait_send()
+    for copy in other_traces:
+        copy.wait_send()
     mate.wait_send()
     norms.wait_send()
     only(has_prev, before.wait_send)
@@ -430,7 +440,7 @@
             pltpu.VMEM((taps, lags), f32),
             pltpu.VMEM((taps, lags), f32),
             pltpu.SemaphoreType.DMA,
-            pltpu.SemaphoreType.DMA((3,)),
+            pltpu.SemaphoreType.DMA((1 + 2 * nblocks,)),
             pltpu.SemaphoreType.DMA((3,)),
             pltpu.SemaphoreType.DMA((4, half, chips)),
             pltpu.SemaphoreType.DMA((half, chips)),

time: 35.4 us -> 36.1 us (1.020)
  Pallas kernels: 33.8 us -> 34.5 us
    pallas_call x1, Pallas kernels: 33.8 us -> 34.5 us  [fused(): pl.pallas_call(functools.partial(kernel, tm), out_shape=jax.ShapeDtypeStr...]
where the time goes in v5:
time: 36.1 us; the launch traced here: 35.9 us
  Pallas kernels  34.5 us (96%)
  local copies, waits for them, and re-layouts  1.47 us (4%)
    pallas_call x1, Pallas kernels, fused(): pl.pallas_call(functools.partial(kernel, tm), out_shape=jax.ShapeDtypeStr...  34.5 us
    unnamed x1, local copies, waits for them, and re-layouts  1.47 us

profile of v5, /device:TPU:1, one launch (start us, length us, event | category | flops | bytes accessed | tf_op | source)
XLA Modules:
  0.0 35.9 jit_solution(12304231332487780066)
XLA Ops:
  0.0 34.5 %shard_map.37 = f32[16,1024]{1,0:T(8,128)} custom-call(s32[4,16]{1,0:T(4,128)} %bitcast.3, bf16[8,128,1024]{2,1,0:T(8,128)(2,1)} %bitcast.2, bf16[16,16,512]{2,1,0:T(8,128)(2,1)} %templates.1), custom_call_target="tpu_custom_call" | custom-call | tf_op jit(solution)/shard_map/pallas_call | solution.py:417
  34.5 1.5 %copy.5 = f32[16,1024]{1,0:T(8,128)} copy(f32[16,1024]{1,0:T(8,128)} %shard_map.37) | data formatting | bytes 131072
